TPU v7x, 256 devices: a whole 4x4x8 slice. The times are simulated.
256 devices in a mesh: space: 32 (over y, z), tm: 8 (over x, core).
Axes of the slice: x: 4, y: 4, z: 8, core: 2. Of those that a mesh axis runs over, the one named last changes fastest.
Arguments:
- fine_residual: bfloat16 [16, 64, 4, 8, 32, 128], P('tm', 'space'), may hold values from -12 to 12
- restriction: bfloat16 [16, 64, 4, 8, 128, 128], P('tm', 'space'), may hold values from -0.25 to 0.25
- coarse_links: bfloat16 [8, 32, 2, 4, 9, 128, 128], P('tm', 'space'), may hold values from -1 to 12.5
- plane_owner: int32 [32], replicated, may hold values from 0 to 31, as said below
Outputs:
- correction: float32 [16, 64, 4, 8, 32, 128], P('tm', 'space')
- coarse_residual: float32 [8, 32, 2, 4, 32, 128], P('tm', 'space')
Inputs may be any that keep to these rules, and one draw needn't show every extreme that they name: `plane_owner`: every coarse plane is named by exactly one owner, and for some plane z the owner at index (z + 16) mod 32 names z.
All inputs are finite; a program needn't handle non-finite values.
Results may differ from a plain program's by a relative error of at most 0.009.
Values may be sent and summed in bfloat16 or wider, within the bound.
A program may use at most 64 MiB of HBM per device.

v0:
```python
import jax
import jax.numpy as jnp
from jax import lax
from jax.sharding import PartitionSpec as P

ITERS = 3


def extended(block, sides, width):
    for axis, dim in sides:
        count = lax.axis_size(axis)
        forward = [(i, i + 1) for i in range(count - 1)]
        forward.append((count - 1, 0))
        backward = [(target, source) for source, target in forward]
        low = lax.ppermute(
            lax.slice_in_dim(block, block.shape[dim] - width, None, axis=dim), axis, forward
        )
        high = lax.ppermute(lax.slice_in_dim(block, 0, width, axis=dim), axis, backward)
        block = jnp.concatenate([low, block, high], axis=dim)
    return block


def inner_sum(left, right):
    return jnp.sum(left * right, axis=(0, 1, 2, 3, 5))


def coarse_apply(vector, links):
    padded = extended(vector, (("tm", 0), ("space", 1)), 1)
    neighbours = [
        vector,
        padded[2:, 1:2],
        padded[:-2, 1:2],
        padded[1:-1, 2:3],
        padded[1:-1, 0:1],
        jnp.roll(vector, -1, 2),
        jnp.roll(vector, 1, 2),
        jnp.roll(vector, -1, 3),
        jnp.roll(vector, 1, 3),
    ]
    stacked = jnp.concatenate(neighbours, axis=-1)
    site_total = vector.shape[0] * vector.shape[1] * vector.shape[2] * vector.shape[3]
    rhs_count = vector.shape[4]
    channels = vector.shape[5]
    flattened = stacked.reshape(site_total, rhs_count, 9 * channels)
    weights = links.reshape(site_total, 9 * channels, channels)
    result = jnp.einsum("snk,ski->sni", flattened, weights, preferred_element_type=jnp.float32)
    return result.reshape(vector.shape)


def collect_plane(plane_block, anchor):
    gathered = lax.all_gather(plane_block, "space", axis=1, tiled=True)
    return lax.dynamic_slice_in_dim(gathered, anchor, 1, 1)


def body(fine_residual, restriction, coarse_links, plane_owner):
    shape_fine = fine_residual.shape
    time_coarse = shape_fine[0] // 2
    rows_y = shape_fine[2] // 2
    rows_x = shape_fine[3] // 2
    rhs_count = shape_fine[4]
    channels = shape_fine[5]
    fine_total = shape_fine[0] * shape_fine[1] * shape_fine[2] * shape_fine[3]
    maps_flat = restriction.reshape(fine_total, channels, channels)
    products = jnp.einsum(
        "snj,sji->sni",
        fine_residual.reshape(fine_total, rhs_count, channels),
        maps_flat,
        preferred_element_type=jnp.float32,
    )
    owner_block = jnp.sum(
        products.reshape(time_coarse, 2, 1, 2, rows_y, 2, rows_x, 2, rhs_count, channels),
        axis=(1, 3, 5, 7),
    )
    planes = lax.axis_size("space")
    myself = lax.axis_index("space")
    seats = jnp.arange(planes, dtype=jnp.int32)
    source = jnp.sum(jnp.where(plane_owner[:, None] == seats[None, :], seats[:, None], 0), axis=0)
    my_source = jnp.sum(jnp.where(seats == myself, source, 0))
    my_plane = jnp.sum(jnp.where(seats == myself, plane_owner, 0))
    residual = collect_plane(owner_block, my_source)
    solution = jnp.zeros_like(residual)
    basis_dirs = []
    basis_imgs = []
    basis_norms = []
    for iteration in range(ITERS):
        direction = residual.astype(jnp.bfloat16)
        images = coarse_apply(direction, coarse_links)
        search = direction.astype(jnp.float32)
        search_img = images
        factors = []
        if iteration > 0:
            projections = lax.psum(
                jnp.stack([inner_sum(basis_imgs[earlier], images) for earlier in range(iteration)]),
                ("space", "tm"),
            )
            factors = [projections[earlier] / basis_norms[earlier] for earlier in range(iteration)]
        for earlier in range(iteration):
            search = search - factors[earlier][:, None] * basis_dirs[earlier]
            search_img = search_img - factors[earlier][:, None] * basis_imgs[earlier]
        norm_now, along = lax.psum(
            (inner_sum(search_img, search_img), inner_sum(search_img, residual)), ("space", "tm")
        )
        step_size = along / norm_now
        solution = solution + step_size[:, None] * search
        residual = residual - step_size[:, None] * search_img
        basis_dirs.append(search)
        basis_imgs.append(search_img)
        basis_norms.append(norm_now)
    owner_fix = collect_plane(solution, my_plane)
    fix_block = owner_fix.astype(jnp.bfloat16)
    expanded = jnp.broadcast_to(
        fix_block.reshape(time_coarse, 1, 1, 1, rows_y, 1, rows_x, 1, rhs_count, channels),
        (time_coarse, 2, 1, 2, rows_y, 2, rows_x, 2, rhs_count, channels),
    ).reshape(fine_total, rhs_count, channels)
    correction = jnp.einsum(
        "sni,sji->snj", expanded, maps_flat, preferred_element_type=jnp.float32
    ).reshape(shape_fine)
    return (correction, residual)


def solution(mesh):
    placed = (
        P("tm", "space", None, None, None, None),
        P("tm", "space", None, None, None, None),
        P("tm", "space", None, None, None, None, None),
        P(),
    )
    return jax.shard_map(
        body,
        mesh=mesh,
        in_specs=placed,
        out_specs=(
            P("tm", "space", None, None, None, None),
            P("tm", "space", None, None, None, None),
        ),
        check_vma=False,
    )
```

profile of v0, /device:TPU:1, one launch (start us, length us, event | category | flops | bytes accessed | tf_op | source)
XLA Modules:
  0.0 607.0 jit_solution(4532591948645891060)
XLA Ops:
  7.2 0.0 copy-start
  7.2 0.0 all-gather.6.cloned.1.call-start
  7.2 5.2 fusion.18
  12.4 0.0 copy-start.1
  12.4 2.4 reduce_sum.119
  14.8 0.0 all-gather.6.cloned.1.call-update
  14.9 0.0 all-gather.4.cloned.1.call-start
  14.9 0.0 copy-done.1
  14.9 0.1 select_reduce_fusion
  15.0 0.6 fusion.7
  17.6 80.4 %all-gather.6.cloned.1.call-done = f32[64,4,32,128]{3,2,1,0:T(8,128)} async-done(((f32[2,4,32,128]{3,2,1,0:T(8,128)}), f32[64,4,32,128]{3,2,1,0:T(8,128)}) %all-gather.6.cloned.1.call-update) | async-done | bytes 4194320 | tf_op jit(solution)/shard_map/all_gather | solution.py:51
  98.0 0.9 constant_dynamic-update-slice_fusion.4
  98.9 3.3 collective-permute-start
  102.2 1.1 collective-permute-start.1
  103.4 1.9 collective-permute-done
  105.3 0.0 collective-permute-done.1
  105.3 2.7 collective-permute-start.2
  108.0 0.0 collective-permute-start.3
  108.0 2.6 collective-permute-done.2
  110.6 5.2 collective-permute-done.3
  115.9 0.0 copy-done
  115.9 0.6 multiply_reduce_fusion.7
  116.5 1.0 multiply_reduce_fusion.8
  117.6 75.1 %all-reduce.2 = (f32[32]{0:T(128)S(1)}, f32[32]{0:T(128)S(1)}) all-reduce(f32[32]{0:T(128)S(1)} %multiply_reduce_fusion.8, f32[32]{0:T(128)S(1)} %get-tuple-element.42), channel_id=1, replica_groups=mesh['space'=32,'tm'=8] {'space','tm'}, use_global_device_ids=true, to_apply=%region_4.5 | all-reduce | flops 64 | bytes 512 | tf_op jit(solution)/shard_map/psum | solution.py:100
  192.7 1.0 constant_dynamic-update-slice_fusion.9
  193.7 0.7 collective-permute-start.4
  194.4 1.1 collective-permute-start.5
  195.5 1.9 collective-permute-done.4
  197.4 0.0 collective-permute-done.5
  197.4 2.8 collective-permute-start.6
  200.2 0.0 collective-permute-start.7
  200.2 2.6 collective-permute-done.6
  202.8 5.2 collective-permute-done.7
  208.2 0.6 multiply_reduce_fusion.6
  208.8 74.6 %psum.58 = f32[32]{0:T(128)S(1)} all-reduce(f32[32]{0:T(128)S(1)} %get-tuple-element.44), channel_id=1, replica_groups=mesh['space'=32,'tm'=8] {'space','tm'}, use_global_device_ids=true, to_apply=%region_8.9 | all-reduce | flops 32 | bytes 256 | tf_op jit(solution)/shard_map/psum | solution.py:92
  283.4 0.2 multiply_reduce_fusion.4
  283.6 0.1 multiply_subtract_fusion.3
  283.7 0.1 multiply_reduce_fusion.5
  283.8 74.3 %all-reduce.1 = (f32[32]{0:T(128)S(1)}, f32[32]{0:T(128)S(1)}) all-reduce(f32[32]{0:T(128)S(1)} %multiply_reduce_fusion.5, f32[32]{0:T(128)S(1)} %multiply_reduce_fusion.4), channel_id=1, replica_groups=mesh['space'=32,'tm'=8] {'space','tm'}, use_global_device_ids=true, to_apply=%region_10.11 | all-reduce | flops 64 | bytes 512 | tf_op jit(solution)/shard_map/psum | solution.py:100
  358.1 0.1 constant_dynamic-update-slice_fusion.14
  358.2 0.7 collective-permute-start.8
  358.9 1.1 collective-permute-start.9
  360.0 1.9 collective-permute-done.8
  361.9 0.0 collective-permute-done.9
  361.9 2.9 collective-permute-start.10
  364.9 0.0 collective-permute-start.11
  364.9 2.6 collective-permute-done.10
  367.5 5.2 collective-permute-done.11
  372.8 0.6 multiply_reduce_fusion.3
  373.4 74.8 %psum.61 = f32[2,32]{1,0:T(2,128)S(1)} all-reduce(f32[2,32]{1,0:T(2,128)S(1)} %pad_maximum_fusion.6), channel_id=1, replica_groups=mesh['space'=32,'tm'=8] {'space','tm'}, use_global_device_ids=true, to_apply=%region_15.16 | all-reduce | flops 64 | bytes 512 | tf_op jit(solution)/shard_map/psum | solution.py:92
  448.3 0.2 multiply_reduce_fusion
  448.5 0.1 multiply_subtract_fusion
  448.6 0.1 multiply_reduce_fusion.1
  448.7 74.3 %all-reduce = (f32[32]{0:T(128)S(1)}, f32[32]{0:T(128)S(1)}) all-reduce(f32[32]{0:T(128)S(1)} %multiply_reduce_fusion.1, f32[32]{0:T(128)S(1)} %multiply_reduce_fusion), channel_id=1, replica_groups=mesh['space'=32,'tm'=8] {'space','tm'}, use_global_device_ids=true, to_apply=%region_17.18 | all-reduce | flops 64 | bytes 512 | tf_op jit(solution)/shard_map/psum | solution.py:100
  523.0 0.8 fusion.1
  523.8 0.0 all-gather.4.cloned.1.call-update
  523.8 0.6 fusion.8
  526.4 0.7 subtract_bitcast_fusion
  527.1 66.2 %all-gather.4.cloned.1.call-done = bf16[1,32,2,4,32,128]{5,4,3,2,0,1:T(8,128)(2,1)} async-done(((bf16[1,1,2,4,32,128]{5,4,3,2,0,1:T(8,128)(2,1)}), bf16[1,32,2,4,32,128]{5,4,3,2,0,1:T(8,128)(2,1)}) %all-gather.4.cloned.1.call-update) | async-done | bytes 2097168 | tf_op jit(solution)/shard_map/all_gather | solution.py:51
  593.3 0.8 fusion.6
  594.2 0.2 broadcast_in_dim.33
  594.4 5.8 fusion.19
  (42 shorter events, 0.6 us)
Async XLA Ops:
  7.2 108.8 %copy-start = (bf16[1,1,2,4,9,128,128]{6,5,4,3,2,1,0:T(8,128)(2,1)S(1)}, bf16[1,1,2,4,9,128,128]{6,5,4,3,2,1,0:T(8,128)(2,1)}, u32[]{:S(2)}) copy-start(bf16[1,1,2,4,9,128,128]{6,5,4,3,2,1,0:T(8,128)(2,1)} %param.6) | copy-start | bytes 7077892
  7.2 90.8 %all-gather.6.cloned.1.call-start = ((), (), s32[]{:S(2)}) async-start(), calls=%async_computation.1 | async-start | bytes 4325376 | tf_op jit(solution)/shard_map/all_gather | solution.py:51
  12.4 2.5 copy-start.1
  14.9 578.5 %all-gather.4.cloned.1.call-start = ((), (), s32[]{:S(2)}) async-start(), calls=%async_computation | async-start | bytes 2162688 | tf_op jit(solution)/shard_map/all_gather | solution.py:51
  98.9 6.3 %collective-permute-start = (bf16[1,1,2,4,32,128]{5,4,3,2,0,1:T(8,128)(2,1)S(1)}, bf16[1,1,2,4,32,128]{5,4,3,2,0,1:T(8,128)(2,1)S(1)}, u32[]{:S(2)}, u32[]{:S(2)}) collective-permute-start(bf16[1,1,2,4,32,128]{5,4,3,2,0,1:T(8,128)(2,1)S(1)} %get-tuple-element.21), channel_id=1, source_target_pairs={{1,0},{2,1},{3,2},{4,3},{5,4},{6,5},{7,6},{0,7},{9,8},{10,9},{11,1... | collective-permute-start | bytes 196616 | tf_op jit(solution)/shard_map/ppermute | solution.py:18
  102.2 3.0 collective-permute-start.1
  105.3 5.3 collective-permute-start.2
  108.0 7.8 %collective-permute-start.3 = (bf16[3,1,2,4,32,128]{5,4,3,2,0,1:T(8,128)(2,1)S(1)}, bf16[3,1,2,4,32,128]{5,4,3,2,0,1:T(8,128)(2,1)S(1)}, u32[]{:S(2)}, u32[]{:S(2)}) collective-permute-start(bf16[3,1,2,4,32,128]{5,4,3,2,0,1:T(8,128)(2,1)S(1)} %pad_maximum_fusion), channel_id=1, source_target_pairs={{0,8},{8,16},{16,24},{24,32},{32,40},{40,48},{48,56},{56,64},{64,7... | collective-permute-start | bytes 589832 | tf_op jit(solution)/shard_map/ppermute | solution.py:15
  193.7 3.7 collective-permute-start.4
  194.4 3.0 collective-permute-start.5
  197.4 5.4 collective-permute-start.6
  200.2 7.8 %collective-permute-start.7 = (bf16[3,1,2,4,32,128]{5,4,3,2,0,1:T(8,128)(2,1)S(1)}, bf16[3,1,2,4,32,128]{5,4,3,2,0,1:T(8,128)(2,1)S(1)}, u32[]{:S(2)}, u32[]{:S(2)}) collective-permute-start(bf16[3,1,2,4,32,128]{5,4,3,2,0,1:T(8,128)(2,1)S(1)} %pad_maximum_fusion.1), channel_id=1, source_target_pairs={{0,8},{8,16},{16,24},{24,32},{32,40},{40,48},{48,56},{56,64},{64,7... | collective-permute-start | bytes 589832 | tf_op jit(solution)/shard_map/ppermute | solution.py:15
  358.2 3.7 collective-permute-start.8
  358.9 3.0 collective-permute-start.9
  361.9 5.5 collective-permute-start.10
  364.9 7.8 %collective-permute-start.11 = (bf16[3,1,2,4,32,128]{5,4,3,2,0,1:T(8,128)(2,1)S(1)}, bf16[3,1,2,4,32,128]{5,4,3,2,0,1:T(8,128)(2,1)S(1)}, u32[]{:S(2)}, u32[]{:S(2)}) collective-permute-start(bf16[3,1,2,4,32,128]{5,4,3,2,0,1:T(8,128)(2,1)S(1)} %pad_maximum_fusion.2), channel_id=1, source_target_pairs={{0,8},{8,16},{16,24},{24,32},{32,40},{40,48},{48,56},{56,64},{64,7... | collective-permute-start | bytes 589832 | tf_op jit(solution)/shard_map/ppermute | solution.py:15
Sparse Core Ops, SparseCore 0:
  15.0 82.9 all-gather.5
  523.9 69.3 all-gather.3
where the time goes:
time: 611 us; the launch traced here: 607 us
  blocking collectives  373 us (61%)
  waiting for transfers between devices  176 us (29%)
  between operations  18.2 us (3%)
  starting transfers between devices  16.4 us (3%)
  matrix products  12.8 us (2%)
  other arithmetic  8.64 us (1%)
    psum x3, blocking collectives, body(): lax.psum((inner_sum(search_img, search_img), inner_sum(search_img, residu...  224 us
    psum x2, blocking collectives, body(): lax.psum(jnp.stack([inner_sum(basis_imgs[earlier], images) for earlier in...  149 us
    all_gather x2, waiting for transfers between devices, collect_plane(): gathered = lax.all_gather(plane_block, 'space', axis=1, tiled=True)  147 us
    ppermute x6, waiting for transfers between devices, extended(): lax.ppermute(lax.slice_in_dim(block, block.shape[dim] - width, None, axis...  15.6 us
    ppermute x6, waiting for transfers between devices, extended(): lax.ppermute(lax.slice_in_dim(block, 0, width, axis=dim), axis, backward)  13.4 us
    ppermute x6, starting transfers between devices, extended(): lax.ppermute(lax.slice_in_dim(block, 0, width, axis=dim), axis, backward)  13.1 us
  transfers between devices with their start and end apart: 14, of which 11 were waited for; matrix products, arithmetic and copies ran while one was open for 0% of the time, Pallas kernels for 0%

commit v1 on v0

v1 whole, which is shorter than its diff:
```python
import jax
import jax.numpy as jnp
from jax import lax
from jax.experimental import pallas as pl
from jax.experimental.pallas import tpu as pltpu
from jax.sharding import PartitionSpec as P

ITERS = 3
NS = 32
NT = 8
NZ = 8
CS = 8
RHS = 32
W = 128
F32 = jnp.float32
BF16 = jnp.bfloat16
MESH = pl.DeviceIdType.MESH


def dot(a, b):
    return jnp.dot(a, b, preferred_element_type=F32)


def kernel(
    owner_ref, fine_ref, restr_ref, links_ref, corr_ref, res_ref,
    fine_v, restr_v, links_v, out_v,
    own_v, mid_v, pick_v, r_v, p_v, halo_v, img_v,
    midb_v, pickb_v, back_v, part_v, sumt_v, sums_v, source_s,
    fine_sem, restr_sem, links_sem, out_sem,
    up_send, up_recv, down_send, down_recv,
    halo_send, halo_recv, t_send, t_recv, s_send, s_recv,
    b1_send, b1_recv, b2_send, b2_recv,
):
    me = lax.axis_index("space")
    tm = lax.axis_index("tm")
    my_y, my_z = me // NZ, me % NZ

    def site_of(step):
        return lax.rem(my_z + 1 + step, CS)

    def fine_copies(step):
        cs = site_of(step)
        y, x = cs // 4, cs % 4
        sl = (slice(None), slice(None), pl.ds(2 * y, 2), pl.ds(2 * x, 2))
        return (
            pltpu.make_async_copy(fine_ref.at[sl], fine_v.at[cs], fine_sem.at[step]),
            pltpu.make_async_copy(restr_ref.at[sl], restr_v.at[cs], restr_sem.at[step]),
        )

    for step in range(CS):
        for c in fine_copies(step):
            c.start()
    links_copy = pltpu.make_async_copy(links_ref.at[0, 0], links_v, links_sem)
    links_copy.start()

    barrier = pltpu.get_barrier_semaphore()
    for d in range(1, NS):
        pl.semaphore_signal(
            barrier, inc=1, device_id={"space": lax.rem(me + d, NS)}, device_id_type=MESH)
    for d in range(1, NT):
        pl.semaphore_signal(
            barrier, inc=1, device_id={"tm": lax.rem(tm + d, NT)}, device_id_type=MESH)

    def find(z, carry):
        acc = jnp.int32(0)
        for s in range(NS):
            acc = jnp.where(owner_ref[s] == z, s, acc)
        source_s[z] = acc
        return carry

    lax.fori_loop(0, NS, find, 0)
    pl.semaphore_wait(barrier, NS - 1 + NT - 1)

    for step in range(CS):
        for c in fine_copies(step):
            c.wait()
        cs = site_of(step)
        acc = jnp.zeros((RHS, W), F32)
        for a in range(2):
            for b in range(2):
                for c in range(2):
                    lhs = jnp.concatenate(
                        [fine_v[cs, a, b, c, 0], fine_v[cs, a, b, c, 1]], axis=-1)
                    acc = acc + dot(lhs, restr_v[cs, a, b, c].reshape(2 * W, W))
        own_v[pl.ds(cs * 4, 4)] = acc.reshape(4, 8, W)
        for q in range(4):
            target = q * NZ + cs

            def send(q=q, target=target, cs=cs):
                pltpu.make_async_remote_copy(
                    src_ref=own_v.at[cs * 4 + q], dst_ref=mid_v.at[me],
                    send_sem=up_send, recv_sem=up_recv,
                    device_id={"space": target}, device_id_type=MESH).start()

            if step < CS - 1:
                send()
            else:
                pl.when(q != my_y)(send)
    my_slot = my_z * 4 + my_y
    mid_v[me] = own_v[my_slot]

    def drain(ref, sem):
        pltpu.make_async_copy(ref, ref, sem).wait()

    others = pl.ds(0, NS - 1)
    drain(mid_v.at[others], up_recv)

    for d in range(1, NS):
        target = lax.rem(me + d, NS)
        pick_v[d] = mid_v[source_s[target]]
        pltpu.make_async_remote_copy(
            src_ref=pick_v.at[d], dst_ref=r_v.at[my_slot],
            send_sem=down_send, recv_sem=down_recv,
            device_id={"space": target}, device_id_type=MESH).start()
    r_v[my_slot] = mid_v[source_s[me]]
    drain(r_v.at[others], down_recv)
    links_copy.wait()

    lane = lax.broadcasted_iota(jnp.int32, (RHS, W), 1)
    row = lax.broadcasted_iota(jnp.int32, (RHS, W), 0)

    def read_r(cs):
        return r_v[pl.ds(4 * cs, 4)].reshape(RHS, W)

    def back_up(it):
        for h in range(16):
            target = 2 * h + it - 1

            @pl.when(target != me)
            def _():
                pltpu.make_async_remote_copy(
                    src_ref=p_v.at[it, h // 2, pl.ds(16 * (h % 2), 16)],
                    dst_ref=midb_v.at[me],
                    send_sem=b1_send.at[it - 1], recv_sem=b1_recv,
                    device_id={"space": target}, device_id_type=MESH).start()

            @pl.when(target == me)
            def _():
                midb_v[me] = p_v[it, h // 2, pl.ds(16 * (h % 2), 16)]

    def back_down(it):
        @pl.when(me % 2 == it - 1)
        def _():
            drain(midb_v.at[others], b1_recv)
            piece = me // 2
            for d in range(1, NS):
                target = lax.rem(me + d, NS)
                pickb_v[d] = midb_v[owner_ref[target]]
                pltpu.make_async_remote_copy(
                    src_ref=pickb_v.at[d], dst_ref=back_v.at[it - 1, piece],
                    send_sem=b2_send, recv_sem=b2_recv.at[it - 1],
                    device_id={"space": target}, device_id_type=MESH).start()
            back_v[it - 1, piece] = midb_v[owner_ref[me]]

    halo_to = (
        {"tm": lax.rem(tm + NT - 1, NT)}, {"tm": lax.rem(tm + 1, NT)},
        {"space": lax.rem(me + NS - 1, NS)}, {"space": lax.rem(me + 1, NS)},
    )

    def halo_copy(it, k):
        return pltpu.make_async_remote_copy(
            src_ref=p_v.at[it], dst_ref=halo_v.at[it, k],
            send_sem=halo_send.at[it, k], recv_sem=halo_recv.at[it, k],
            device_id=halo_to[k], device_id_type=MESH)

    norms, alphas, betas = [], [], []
    for it in range(ITERS):
        for cs in range(CS):
            p_v[it, cs] = read_r(cs).astype(BF16)
        for k in range(4):
            halo_copy(it, k).start()
        if it > 0:
            back_up(it)
        for cs in range(CS):
            y, x = cs // 4, cs % 4
            vy = p_v[it, (1 - y) * 4 + x]
            lhs = jnp.concatenate(
                [vy, vy, p_v[it, y * 4 + (x + 1) % 4], p_v[it, y * 4 + (x + 3) % 4]], axis=-1)
            img_v[it, cs] = dot(lhs, links_v[y, x, pl.ds(5, 4)].reshape(4 * W, W)) + dot(
                p_v[it, cs], links_v[y, x, 0])
        for k in range(4):
            halo_copy(it, k).wait_recv()
        nprod = it + 2
        prods = [jnp.zeros((RHS, W), F32) for _ in range(nprod)]
        for cs in range(CS):
            y, x = cs // 4, cs % 4
            lhs = jnp.concatenate([halo_v[it, k, cs] for k in range(4)], axis=-1)
            q = img_v[it, cs] + dot(lhs, links_v[y, x, pl.ds(1, 4)].reshape(4 * W, W))
            img_v[it, cs] = q
            factors = [img_v[j, cs] for j in range(it)] + [q, read_r(cs)]
            for k in range(nprod):
                prods[k] = prods[k] + q * factors[k]
        packed = jnp.zeros((RHS, W), F32)
        for k in range(nprod):
            total = jnp.sum(prods[k], axis=1, keepdims=True)
            packed = packed + jnp.where(lane == row + RHS * k, total, 0.0)
        mine = jnp.sum(packed, axis=0, keepdims=True)

        part_v[it, 0] = mine
        sumt_v[it, tm] = mine
        for d in range(1, NT):
            pltpu.make_async_remote_copy(
                src_ref=part_v.at[it, 0], dst_ref=sumt_v.at[it, tm],
                send_sem=t_send.at[it], recv_sem=t_recv.at[it],
                device_id={"tm": lax.rem(tm + d, NT)}, device_id_type=MESH).start()
        if it > 0:
            back_down(it)
        drain(sumt_v.at[it, pl.ds(0, NT - 1)], t_recv.at[it])
        over_t = jnp.sum(sumt_v[it], axis=0)
        part_v[it, 1] = over_t
        sums_v[it, me] = over_t
        for d in range(1, NS):
            pltpu.make_async_remote_copy(
                src_ref=part_v.at[it, 1], dst_ref=sums_v.at[it, me],
                send_sem=s_send.at[it], recv_sem=s_recv.at[it],
                device_id={"space": lax.rem(me + d, NS)}, device_id_type=MESH).start()
        drain(sums_v.at[it, others], s_recv.at[it])
        totals = jnp.broadcast_to(jnp.sum(sums_v[it], axis=0), (RHS, W))
        cols = [
            jnp.sum(jnp.where(lane == row + RHS * k, totals, 0.0), axis=1, keepdims=True)
            for k in range(nprod)
        ]
        beta = [cols[j] / norms[j] for j in range(it)]
        norm = cols[it]
        for j in range(it):
            norm = norm - beta[j] * cols[j]
        alpha = cols[it + 1] / norm
        norms.append(norm)
        alphas.append(alpha)
        betas.append(beta)
        for cs in range(CS):
            q = img_v[it, cs]
            for j in range(it):
                q = q - beta[j] * img_v[j, cs]
            img_v[it, cs] = q
            new = read_r(cs) - alpha * q
            if it < ITERS - 1:
                r_v[pl.ds(4 * cs, 4)] = new.reshape(4, 8, W)
            else:
                res_ref[0, 0, cs // 4, cs % 4] = new

    c2 = alphas[2]
    c1 = alphas[1] - alphas[2] * betas[2][1]
    c0 = alphas[0] - c1 * betas[1][0] - alphas[2] * betas[2][0]

    for it in (1, 2):
        @pl.when(me % 2 == it - 1)
        def _():
            drain(back_v.at[it - 1, pl.ds(0, 15)], b2_recv.at[it - 1])

        @pl.when(me % 2 != it - 1)
        def _():
            drain(back_v.at[it - 1], b2_recv.at[it - 1])

    out_copies = []
    for cs in range(CS):
        y, x = cs // 4, cs % 4
        own = own_v[pl.ds(4 * cs, 4)].reshape(RHS, W).astype(BF16).astype(F32)
        d1 = back_v[0, pl.ds(2 * cs, 2)].reshape(RHS, W).astype(F32)
        d2 = back_v[1, pl.ds(2 * cs, 2)].reshape(RHS, W).astype(F32)
        fix = (c0 * own + c1 * d1 + c2 * d2).astype(BF16)
        for a in range(2):
            for b in range(2):
                for c in range(2):
                    both = lax.dot_general(
                        fix, restr_v[cs, a, b, c].reshape(2 * W, W),
                        (((1,), (1,)), ((), ())), preferred_element_type=F32)
                    out_v[cs, a, b, c, 0] = both[:, :W]
                    out_v[cs, a, b, c, 1] = both[:, W:]
        copy = pltpu.make_async_copy(
            out_v.at[cs],
            corr_ref.at[:, :, pl.ds(2 * y, 2), pl.ds(2 * x, 2)], out_sem.at[cs])
        copy.start()
        out_copies.append(copy)

    drain(own_v.at[others], up_send)
    drain(pick_v.at[others], down_send)
    for it in range(ITERS):
        for k in range(4):
            halo_copy(it, k).wait_send()
        drain(sumt_v.at[it, pl.ds(0, NT - 1)], t_send.at[it])
        drain(sums_v.at[it, others], s_send.at[it])
    for it in (1, 2):
        @pl.when(me % 2 == it - 1)
        def _():
            drain(back_v.at[it - 1, pl.ds(0, 15)], b1_send.at[it - 1])

        @pl.when(me % 2 != it - 1)
        def _():
            drain(back_v.at[it - 1], b1_send.at[it - 1])
    drain(pickb_v.at[others], b2_send)
    for copy in out_copies:
        copy.wait()


def body(fine_residual, restriction, coarse_links, plane_owner):
    dma = pltpu.SemaphoreType.DMA
    anyspec = pl.BlockSpec(memory_space=pl.ANY)
    return pl.pallas_call(
        kernel,
        out_shape=(
            jax.ShapeDtypeStruct(fine_residual.shape, F32),
            jax.ShapeDtypeStruct((1, 1, 2, 4, RHS, W), F32),
        ),
        in_specs=[pl.BlockSpec(memory_space=pltpu.SMEM), anyspec, anyspec, anyspec],
        out_specs=(anyspec, pl.BlockSpec(memory_space=pltpu.VMEM)),
        scratch_shapes=[
            pltpu.VMEM((CS, 2, 2, 2, 2, RHS, W), BF16),
            pltpu.VMEM((CS, 2, 2, 2, 2, W, W), BF16),
            pltpu.VMEM((2, 4, 9, W, W), BF16),
            pltpu.VMEM((CS, 2, 2, 2, 2, RHS, W), F32),
            pltpu.VMEM((NS, 8, W), F32),
            pltpu.VMEM((NS, 8, W), F32),
            pltpu.VMEM((NS, 8, W), F32),
            pltpu.VMEM((NS, 8, W), F32),
            pltpu.VMEM((ITERS, CS, RHS, W), BF16),
            pltpu.VMEM((ITERS, 4, CS, RHS, W), BF16),
            pltpu.VMEM((ITERS, CS, RHS, W), F32),
            pltpu.VMEM((NS, 16, W), BF16),
            pltpu.VMEM((NS, 16, W), BF16),
            pltpu.VMEM((2, 16, 16, W), BF16),
            pltpu.VMEM((ITERS, 2, 1, W), F32),
            pltpu.VMEM((ITERS, NT, 1, W), F32),
            pltpu.VMEM((ITERS, NS, 1, W), F32),
            pltpu.SMEM((NS,), jnp.int32),
            dma((CS,)), dma((CS,)), dma(()), dma((CS,)),
            dma(()), dma(()), dma(()), dma(()),
            dma((ITERS, 4)), dma((ITERS, 4)),
            dma((ITERS,)), dma((ITERS,)), dma((ITERS,)), dma((ITERS,)),
            dma((2,)), dma(()), dma(()), dma((2,)),
        ],
        compiler_params=pltpu.CompilerParams(
            collective_id=0, has_side_effects=True, vmem_limit_bytes=60 * 1024 * 1024),
        name="coarse_correction",
    )(plane_owner, fine_residual, restriction, coarse_links)


def solution(mesh):
    placed = (
        P("tm", "space", None, None, None, None),
        P("tm", "space", None, None, None, None),
        P("tm", "space", None, None, None, None, None),
        P(),
    )
    return jax.shard_map(
        body,
        mesh=mesh,
        in_specs=placed,
        out_specs=(
            P("tm", "space", None, None, None, None),
            P("tm", "space", None, None, None, None),
        ),
        check_vma=False,
    )
```

time: 611 us -> 77.2 us (0.13)
  blocking collectives: 373 us -> 0 us
  waiting for transfers between devices: 176 us -> 0 us
  Pallas kernels: 0 us -> 72.6 us
  between operations: 18.2 us -> 0.65 us
  starting transfers between devices: 16.4 us -> 0 us
  matrix products: 12.8 us -> 0 us
  other arithmetic: 8.64 us -> 0 us
    psum x5 -> x0, blocking collectives: 373 us -> none  [the longest x3 224 us: body(): lax.psum((inner_sum(search_img, search_img), inner_sum(search_img, residu...]
    all_gather x2 -> x0, waiting for transfers between devices: 147 us -> none  [collect_plane(): gathered = lax.all_gather(plane_block, 'space', axis=1, tiled=True)]
    pallas_call x0 -> x1, Pallas kernels: none -> 72.6 us  [body(): pl.pallas_call(kernel, out_shape=(jax.ShapeDtypeStruct(fine_residual.shap...]
    ppermute x12 -> x0, waiting for transfers between devices: 29 us -> none  [the longest x6 15.6 us: extended(): lax.ppermute(lax.slice_in_dim(block, block.shape[dim] - width, None, axis...]
    ppermute x12 -> x0, starting transfers between devices: 16.3 us -> none  [the longest x6 13.1 us: extended(): lax.ppermute(lax.slice_in_dim(block, 0, width, axis=dim), axis, backward)]
    dot_general x5 -> x0, matrix products: 12.8 us -> none  [the longest x1 5.8 us: body(): jnp.einsum('sni,sji->snj', expanded, maps_flat, preferred_element_type=jn...]
  transfers between devices with their start and end apart: 14 -> 0, of which waited for: 11 -> 0; matrix products, arithmetic and copies ran while one was open for 0% -> 0% of each run, Pallas kernels for 0% -> 0%
where the time goes in v1:
time: 77.2 us; the launch traced here: 77.1 us
  Pallas kernels  72.6 us (94%)
  local copies, waits for them, and re-layouts  3.84 us (5%)
    pallas_call x1, Pallas kernels, body(): pl.pallas_call(kernel, out_shape=(jax.ShapeDtypeStruct(fine_residual.shap...  72.6 us
    unnamed x4, local copies, waits for them, and re-layouts  3.84 us

profile of v1, /device:TPU:1, one launch (start us, length us, event | category | flops | bytes accessed | tf_op | source)
XLA Modules:
  0.0 77.1 jit_solution(15446489775171196830)
XLA Ops:
  0.6 72.6 %coarse_correction.1 = (f32[2,2,4,8,32,128]{5,4,3,2,1,0:T(8,128)}, f32[1,1,2,4,32,128]{5,4,3,2,1,0:T(8,128)}) custom-call(s32[32]{0:T(128)} %owner_ref.1, bf16[2,2,4,8,32,128]{5,4,3,2,1,0:T(8,128)(2,1)} %fine_ref.1, bf16[2,2,4,8,128,128]{5,4,3,2,1,0:T(8,128)(2,1)} %restr_ref.1, bf16[1,1,2,4,9,128,128]{6,5,4,3,2,1,0:T(8,128)(2,1)} %links_ref.1), custom_call_target="tpu_custom_call" | custom-call | tf_op jit(solution)/shard_map/coarse_correction/pallas_call | solution.py:299
  73.3 0.0 copy-start
  73.3 3.2 %copy.8 = f32[2,2,4,8,32,128]{5,4,3,2,1,0:T(8,128)} copy(f32[2,2,4,8,32,128]{5,4,3,2,1,0:T(8,128)} %get-tuple-element.4) | data formatting | bytes 4194304
  76.4 0.0 copy-done
  76.5 0.7 copy.9
Async XLA Ops:
  73.3 3.2 %copy-start = (f32[1,1,2,4,32,128]{5,4,3,2,1,0:T(8,128)S(1)}, f32[1,1,2,4,32,128]{5,4,3,2,1,0:T(8,128)}, u32[]{:S(2)}) copy-start(f32[1,1,2,4,32,128]{5,4,3,2,1,0:T(8,128)} %get-tuple-element.5) | copy-start | bytes 393220

commit v2 on v1

v2 whole, which is shorter than its diff:
```python
import jax
import jax.numpy as jnp
from jax import lax
from jax.experimental import pallas as pl
from jax.experimental.pallas import tpu as pltpu
from jax.sharding import PartitionSpec as P

ITERS = 3
NS = 32
NT = 8
NY, NZ = 4, 8
CHIPS = NS * NT // 2
CS = 8
RHS = 32
W = 128
F32 = jnp.float32
BF16 = jnp.bfloat16
MESH = pl.DeviceIdType.MESH
MIB = 1024 * 1024


def dot(a, b):
    return jnp.dot(a, b, preferred_element_type=F32)


def drain(ref, sem):
    pltpu.make_async_copy(ref, ref, sem).wait()


def far_first(i, n):
    return n // 2 + (1 - 2 * (i % 2)) * ((i + 1) // 2)


def cycle_kernel(
    owner_hbm, fine_ref, restr_ref, links_ref, fix_ref, res_ref,
    fine_v, restr_v, links_v, fix_v, res_v,
    own_v, mid_v, pick_v, r_v, low_v, p_v, img_v, orth_v,
    ph_v, lowh_v, imgh_v, rh_v,
    midq0_v, midq1_v, pickq_v, backq_v, part_v, pair_v, sums_v, owner_ref, source_s,
    owner_sem, fix_sem, res_sem, fine_sem, restr_sem, links_sem,
    up_send, up_recv, down_send, down_recv,
    p_send, p_recv, low_send, low_recv, img_send, img_recv,
    c_send, c_recv, s_send, s_recv, b1_send, b1_recv, b2_send, b2_recv,
):
    me = lax.axis_index("space")
    tm = lax.axis_index("tm")
    my_y, my_z = me // NZ, me % NZ
    my_x, my_c = tm // 2, tm % 2

    def space_far(d):
        dz, dy = far_first(d // NY, NZ), far_first(d % NY, NY)
        return lax.rem(my_y + dy, NY) * NZ + lax.rem(my_z + dz, NZ)

    def site_of(step):
        return lax.rem(my_z + far_first(step, NZ), CS)

    def fine_copies(step):
        cs = site_of(step)
        y, x = cs // 4, cs % 4
        sl = (slice(None), slice(None), pl.ds(2 * y, 2), pl.ds(2 * x, 2))
        return (
            pltpu.make_async_copy(fine_ref.at[sl], fine_v.at[cs], fine_sem.at[step]),
            pltpu.make_async_copy(restr_ref.at[sl], restr_v.at[cs], restr_sem.at[step]),
        )

    owner_copy = pltpu.make_async_copy(owner_hbm, owner_ref, owner_sem)
    owner_copy.start()
    for step in range(CS):
        for c in fine_copies(step):
            c.start()
    links_copy = pltpu.make_async_copy(links_ref.at[0, 0], links_v, links_sem)
    links_copy.start()

    barrier = pltpu.get_barrier_semaphore()
    for d in range(1, NS):
        pl.semaphore_signal(
            barrier, inc=1, device_id={"space": lax.rem(me + d, NS)}, device_id_type=MESH)
    for d in range(1, NT):
        pl.semaphore_signal(
            barrier, inc=1, device_id={"tm": lax.rem(tm + d, NT)}, device_id_type=MESH)

    def find(z, carry):
        acc = jnp.int32(0)
        for s in range(NS):
            acc = jnp.where(owner_ref[s] == z, s, acc)
        source_s[z] = acc
        return carry

    owner_copy.wait()
    lax.fori_loop(0, NS, find, 0)

    for step in range(CS):
        for c in fine_copies(step):
            c.wait()
        cs = site_of(step)
        acc = jnp.zeros((RHS, W), F32)
        for a in range(2):
            for b in range(2):
                for c in range(2):
                    lhs = jnp.concatenate(
                        [fine_v[cs, a, b, c, 0], fine_v[cs, a, b, c, 1]], axis=-1)
                    acc = acc + dot(lhs, restr_v[cs, a, b, c].reshape(2 * W, W))
        own_v[pl.ds(cs * 4, 4)] = acc.reshape(4, 8, W)
    pl.semaphore_wait(barrier, NS - 1 + NT - 1)
    my_slot = my_z * 4 + my_y
    others = pl.ds(0, NS - 1)

    def piece(d):
        target = space_far(d)
        return target, target % NZ * 4 + target // NZ

    for d in range(NS - 1):
        target, slot = piece(d)
        pltpu.make_async_remote_copy(
            src_ref=own_v.at[slot], dst_ref=mid_v.at[me],
            send_sem=up_send, recv_sem=up_recv,
            device_id={"space": target}, device_id_type=MESH).start()
    mid_v[me] = own_v[my_slot]
    drain(mid_v.at[others], up_recv)

    for d in range(NS - 1):
        target = space_far(d)
        pick_v[d] = mid_v[source_s[target]]
        pltpu.make_async_remote_copy(
            src_ref=pick_v.at[d], dst_ref=r_v.at[my_slot],
            send_sem=down_send, recv_sem=down_recv,
            device_id={"space": target}, device_id_type=MESH).start()
    r_v[my_slot] = mid_v[source_s[me]]
    drain(r_v.at[others], down_recv)
    links_copy.wait()

    lane = lax.broadcasted_iota(jnp.int32, (RHS, W), 1)
    row = lax.broadcasted_iota(jnp.int32, (RHS, W), 0)

    def read_r(cs):
        return r_v[pl.ds(4 * cs, 4)].reshape(RHS, W)

    def read_img(it, cs):
        return img_v[it, pl.ds(4 * cs, 4)].reshape(RHS, W)

    def put_img(it, cs, q):
        img_v[it, pl.ds(4 * cs, 4)] = q.reshape(4, 8, W)

    def read_imgh(it, k, cs):
        return imgh_v[it, k, pl.ds(4 * cs, 4)].reshape(RHS, W)

    midq = (midq0_v, midq1_v)

    def back_up(it):
        for d in range(NS - 1):
            target, slot = piece(d)
            pltpu.make_async_remote_copy(
                src_ref=img_v.at[it, slot], dst_ref=midq[it].at[me],
                send_sem=b1_send.at[it], recv_sem=b1_recv.at[it],
                device_id={"space": target}, device_id_type=MESH).start()
        midq[it][me] = img_v[it, my_slot]

    def back_down(it):
        drain(midq[it].at[others], b1_recv.at[it])
        for d in range(NS - 1):
            target = space_far(d)
            pickq_v[it, d] = midq[it][owner_ref[target]]
            pltpu.make_async_remote_copy(
                src_ref=pickq_v.at[it, d], dst_ref=backq_v.at[it, my_slot],
                send_sem=b2_send.at[it], recv_sem=b2_recv.at[it],
                device_id={"space": target}, device_id_type=MESH).start()
        backq_v[it, my_slot] = midq[it][owner_ref[me]]

    halo_to = (
        {"tm": lax.rem(tm + NT - 1, NT)}, {"tm": lax.rem(tm + 1, NT)},
        {"space": lax.rem(me + NS - 1, NS)}, {"space": lax.rem(me + 1, NS)},
    )

    def halo_copy(src, dst, send, recv, k):
        return pltpu.make_async_remote_copy(
            src_ref=src, dst_ref=dst, send_sem=send, recv_sem=recv,
            device_id=halo_to[k], device_id_type=MESH)

    p_halo = [halo_copy(p_v.at[0], ph_v.at[0, k], p_send.at[k], p_recv.at[k], k)
              for k in range(4)]
    low_halo = [halo_copy(low_v, lowh_v.at[k], low_send.at[k], low_recv.at[k], k)
                for k in range(4)]
    img_halo = [[halo_copy(img_v.at[it], imgh_v.at[it, k], img_send.at[it, k],
                           img_recv.at[it, k], k) for k in range(4)] for it in range(2)]

    def pair_copy(it):
        return pltpu.make_async_remote_copy(
            src_ref=part_v.at[it, 0], dst_ref=pair_v.at[it, my_c],
            send_sem=c_send.at[it], recv_sem=c_recv.at[it],
            device_id={"tm": my_x * 2 + 1 - my_c}, device_id_type=MESH)

    ring = (2, 1, 3, 0)
    rows_y = [lax.rem(my_y + dy, NY) * NZ for dy in ring]
    cols_x = [lax.rem(my_x + dx, 4) * 2 + my_c for dx in ring]
    chip = me * 4 + my_x

    def send_chip(it):
        def layer(dz, skip):
            z = lax.rem(my_z + dz, NZ)
            for i in range(16 - skip):
                pltpu.make_async_remote_copy(
                    src_ref=part_v.at[it, 1], dst_ref=sums_v.at[it, chip],
                    send_sem=s_send.at[it], recv_sem=s_recv.at[it],
                    device_id={"space": rows_y[i // 4] + z, "tm": cols_x[i % 4]},
                    device_id_type=MESH).start()

        def one(k, carry):
            layer(far_first(k, NZ), 0)
            return carry

        lax.fori_loop(0, NZ - 1, one, 0)
        layer(0, 1)

    norms, alphas, betas = [], [], []
    for it in range(ITERS):
        if it == 0:
            for cs in range(CS):
                p_v[0, cs] = read_r(cs).astype(BF16)
            for k in range(4):
                p_halo[k].start()
            for cs in range(CS):
                low_v[cs] = (read_r(cs) - p_v[0, cs].astype(F32)).astype(BF16)
            for k in range(4):
                low_halo[k].start()

        def inner(cs):
            y, x = cs // 4, cs % 4
            vy = p_v[it, (1 - y) * 4 + x]
            return [vy, vy, p_v[it, y * 4 + (x + 1) % 4], p_v[it, y * 4 + (x + 3) % 4]]

        def outer(cs):
            return [ph_v[it, k, cs] for k in range(4)]

        if it == 0:
            for cs in range(CS):
                y, x = cs // 4, cs % 4
                put_img(it, cs, dot(p_v[it, cs], links_v[y, x, 0]) + dot(
                    jnp.concatenate(inner(cs), axis=-1),
                    links_v[y, x, pl.ds(5, 4)].reshape(4 * W, W)))
            for k in range(4):
                p_halo[k].wait_recv()
        nprod = it + 2
        prods = [jnp.zeros((RHS, W), F32) for _ in range(nprod)]
        for cs in range(CS):
            y, x = cs // 4, cs % 4
            if it == 0:
                q = read_img(it, cs) + dot(
                    jnp.concatenate(outer(cs), axis=-1),
                    links_v[y, x, pl.ds(1, 4)].reshape(4 * W, W))
            else:
                q = dot(
                    jnp.concatenate([p_v[it, cs]] + outer(cs) + inner(cs), axis=-1),
                    links_v[y, x].reshape(9 * W, W))
            put_img(it, cs, q)
            earlier = [read_img(0, cs), orth_v[cs]] if it == 2 else [read_img(0, cs)] * it
            factors = earlier + [q, read_r(cs)]
            for k in range(nprod):
                prods[k] = prods[k] + q * factors[k]
        packed = jnp.zeros((RHS, W), F32)
        for k in range(nprod):
            total = jnp.sum(prods[k], axis=1, keepdims=True)
            packed = packed + jnp.where(lane == row + RHS * k, total, 0.0)
        mine = jnp.sum(packed, axis=0, keepdims=True)

        part_v[it, 0] = mine
        pair_v[it, my_c] = mine
        pair = pair_copy(it)
        pair.start()
        pair.wait_recv()
        both = pair_v[it, 0] + pair_v[it, 1]
        part_v[it, 1] = both
        sums_v[it, chip] = both
        send_chip(it)
        if it < 2:
            for k in range(4):
                img_halo[it][k].start()
        if it > 0:
            back_down(it - 1)
        if it < 2:
            back_up(it)
        drain(sums_v.at[it, pl.ds(0, CHIPS - 1)], s_recv.at[it])
        totals = jnp.broadcast_to(jnp.sum(sums_v[it], axis=0), (RHS, W))
        cols = [
            jnp.sum(jnp.where(lane == row + RHS * k, totals, 0.0), axis=1, keepdims=True)
            for k in range(nprod)
        ]
        beta = [cols[j] / norms[j] for j in range(it)]
        norm = cols[it]
        for j in range(it):
            norm = norm - beta[j] * cols[j]
        alpha = cols[it + 1] / norm
        norms.append(norm)
        alphas.append(alpha)
        betas.append(beta)
        step = jnp.broadcast_to(alpha, (RHS, W))
        coef = [jnp.broadcast_to(b, (RHS, W)) for b in beta]
        for cs in range(CS):
            q = read_img(it, cs)
            if it > 0:
                q = q - coef[0] * read_img(0, cs)
            if it == 1:
                orth_v[cs] = q
            if it == 2:
                q = q - coef[1] * orth_v[cs]
            new = read_r(cs) - step * q
            if it < ITERS - 1:
                r_v[pl.ds(4 * cs, 4)] = new.reshape(4, 8, W)
                p_v[it + 1, cs] = new.astype(BF16)
            else:
                res_v[cs // 4, cs % 4] = new
        if it < ITERS - 1:
            for k in range(4):
                if it == 0:
                    low_halo[k].wait_recv()
                img_halo[it][k].wait_recv()
                for cs in range(CS):
                    q = read_imgh(it, k, cs)
                    if it == 0:
                        old = ph_v[0, k, cs].astype(F32) + lowh_v[k, cs].astype(F32)
                    else:
                        old = rh_v[k, cs]
                        q = q - coef[0] * read_imgh(0, k, cs)
                    new = old - step * q
                    if it == 0:
                        rh_v[k, cs] = new
                    ph_v[it + 1, k, cs] = new.astype(BF16)

    res_copy = pltpu.make_async_copy(res_v, res_ref.at[0, 0], res_sem)
    res_copy.start()

    c2 = alphas[2]
    c1 = alphas[1] - c2 * betas[2][1]
    c0 = alphas[0] - c1 * betas[1][0] - c2 * betas[2][0]

    wide = lambda c: jnp.broadcast_to(c, (RHS, W))
    w0, w1, w2 = wide(c0), wide(c1), wide(c2)
    s0, s1, b10 = wide(alphas[0]), wide(alphas[1]), wide(betas[1][0])
    for it in range(2):
        drain(backq_v.at[it, others], b2_recv.at[it])
    for cs in range(CS):
        sl = pl.ds(4 * cs, 4)
        r0 = own_v[sl].reshape(RHS, W)
        q0 = backq_v[0, sl].reshape(RHS, W)
        r1 = r0 - s0 * q0
        r2 = r1 - s1 * (backq_v[1, sl].reshape(RHS, W) - b10 * q0)
        dirs = [r.astype(BF16).astype(F32) for r in (r0, r1, r2)]
        fix_v[cs] = (w0 * dirs[0] + w1 * dirs[1] + w2 * dirs[2]).astype(BF16)

    fix_copy = pltpu.make_async_copy(fix_v, fix_ref, fix_sem)
    fix_copy.start()

    drain(own_v.at[others], up_send)
    drain(pick_v.at[others], down_send)
    for k in range(4):
        p_halo[k].wait_send()
        low_halo[k].wait_send()
        for it in range(2):
            img_halo[it][k].wait_send()
    for it in range(ITERS):
        pair_copy(it).wait_send()
        drain(sums_v.at[it, pl.ds(0, CHIPS - 1)], s_send.at[it])
    for it in range(2):
        drain(midq[it].at[others], b1_send.at[it])
        drain(pickq_v.at[it, others], b2_send.at[it])
    res_copy.wait()
    fix_copy.wait()


def prolong_kernel(fix_ref, res_in_ref, restr_ref, corr_ref, res_ref,
                   fix_v, restr_v, out_v, fix_sem, res_sem, restr_sem, out_sem):
    def views(cs):
        y, x = cs // 4, cs % 4
        return (slice(None), slice(None), pl.ds(2 * y, 2), pl.ds(2 * x, 2))

    fix_copy = pltpu.make_async_copy(fix_ref, fix_v, fix_sem)
    fix_copy.start()
    loads = [
        pltpu.make_async_copy(restr_ref.at[views(cs)], restr_v.at[cs], restr_sem.at[cs])
        for cs in range(CS)
    ]
    stores = [
        pltpu.make_async_copy(out_v.at[cs], corr_ref.at[views(cs)], out_sem.at[cs])
        for cs in range(CS)
    ]
    for load in loads:
        load.start()
    res_copy = pltpu.make_async_copy(res_in_ref, res_ref, res_sem)
    res_copy.start()
    fix_copy.wait()
    for cs in range(CS):
        loads[cs].wait()
        fix = fix_v[cs]
        for a in range(2):
            for b in range(2):
                for c in range(2):
                    both = lax.dot_general(
                        fix, restr_v[cs, a, b, c].reshape(2 * W, W),
                        (((1,), (1,)), ((), ())), preferred_element_type=F32)
                    out_v[cs, a, b, c, 0] = both[:, :W]
                    out_v[cs, a, b, c, 1] = both[:, W:]
        stores[cs].start()
    res_copy.wait()
    for store in stores:
        store.wait()


def body(fine_residual, restriction, coarse_links, plane_owner):
    dma = pltpu.SemaphoreType.DMA
    hbm = pl.BlockSpec(memory_space=pl.ANY)
    res_shape = jax.ShapeDtypeStruct((1, 1, 2, 4, RHS, W), F32)
    plane = (NS, 8, W)
    fix, res = pl.pallas_call(
        cycle_kernel,
        out_shape=(jax.ShapeDtypeStruct((CS, RHS, W), BF16), res_shape),
        in_specs=[hbm, hbm, hbm, hbm],
        out_specs=(hbm, hbm),
        scratch_shapes=[
            pltpu.VMEM((CS, 2, 2, 2, 2, RHS, W), BF16),
            pltpu.VMEM((CS, 2, 2, 2, 2, W, W), BF16),
            pltpu.VMEM((2, 4, 9, W, W), BF16),
            pltpu.VMEM((CS, RHS, W), BF16),
            pltpu.VMEM((2, 4, RHS, W), F32),
            pltpu.VMEM(plane, F32),
            pltpu.VMEM(plane, F32),
            pltpu.VMEM(plane, F32),
            pltpu.VMEM(plane, F32),
            pltpu.VMEM((CS, RHS, W), BF16),
            pltpu.VMEM((ITERS, CS, RHS, W), BF16),
            pltpu.VMEM((ITERS,) + plane, F32),
            pltpu.VMEM((CS, RHS, W), F32),
            pltpu.VMEM((ITERS, 4, CS, RHS, W), BF16),
            pltpu.VMEM((4, CS, RHS, W), BF16),
            pltpu.VMEM((2, 4) + plane, F32),
            pltpu.VMEM((4, CS, RHS, W), F32),
            pltpu.VMEM(plane, F32),
            pltpu.VMEM(plane, F32),
            pltpu.VMEM((2,) + plane, F32),
            pltpu.VMEM((2,) + plane, F32),
            pltpu.VMEM((ITERS, 2, 1, W), F32),
            pltpu.VMEM((ITERS, 2, 1, W), F32),
            pltpu.VMEM((ITERS, CHIPS, 1, W), F32),
            pltpu.SMEM((NS,), jnp.int32),
            pltpu.SMEM((NS,), jnp.int32),
            dma(()), dma(()), dma(()), dma((CS,)), dma((CS,)), dma(()),
            dma(()), dma(()), dma(()), dma(()),
            dma((4,)), dma((4,)), dma((4,)), dma((4,)), dma((2, 4)), dma((2, 4)),
            dma((ITERS,)), dma((ITERS,)), dma((ITERS,)), dma((ITERS,)),
            dma((2,)), dma((2,)), dma((2,)), dma((2,)),
        ],
        compiler_params=pltpu.CompilerParams(
            collective_id=0, has_side_effects=True, vmem_limit_bytes=60 * MIB),
        name="coarse_cycle",
    )(plane_owner, fine_residual, restriction, coarse_links)
    return pl.pallas_call(
        prolong_kernel,
        out_shape=(jax.ShapeDtypeStruct(fine_residual.shape, F32), res_shape),
        in_specs=[hbm, hbm, hbm],
        out_specs=(hbm, hbm),
        scratch_shapes=[
            pltpu.VMEM((CS, RHS, W), BF16),
            pltpu.VMEM((CS, 2, 2, 2, 2, W, W), BF16),
            pltpu.VMEM((CS, 2, 2, 2, 2, RHS, W), F32),
            dma(()), dma(()), dma((CS,)), dma((CS,)),
        ],
        compiler_params=pltpu.CompilerParams(vmem_limit_bytes=60 * MIB),
        name="prolong",
    )(fix, res, restriction)


def solution(mesh):
    placed = (
        P("tm", "space", None, None, None, None),
        P("tm", "space", None, None, None, None),
        P("tm", "space", None, None, None, None, None),
        P(),
    )
    return jax.shard_map(
        body,
        mesh=mesh,
        in_specs=placed,
        out_specs=(
            P("tm", "space", None, None, None, None),
            P("tm", "space", None, None, None, None),
        ),
        check_vma=False,
    )
```

time: 77.2 us -> 67.6 us (0.88)
  Pallas kernels: 72.6 us -> 66.9 us
  local copies, waits for them, and re-layouts: 3.84 us -> 0 us
    pallas_call x1 -> x2, Pallas kernels: 72.6 us -> 66.9 us  [the longest x1 61.6 us: body(): pl.pallas_call(cycle_kernel, out_shape=(jax.ShapeDtypeStruct((CS, RHS, W)...]
    unnamed x4 -> x0, local copies, waits for them, and re-layouts: 3.84 us -> none
where the time goes in v2:
time: 67.6 us; the launch traced here: 67.5 us
  Pallas kernels  66.9 us (99%)
    pallas_call x1, Pallas kernels, body(): pl.pallas_call(cycle_kernel, out_shape=(jax.ShapeDtypeStruct((CS, RHS, W)...  61.6 us
    pallas_call x1, Pallas kernels, body(): pl.pallas_call(prolong_kernel, out_shape=(jax.ShapeDtypeStruct(fine_resid...  5.28 us

profile of v2, /device:TPU:1, one launch (start us, length us, event | category | flops | bytes accessed | tf_op | source)
XLA Modules:
  0.0 67.5 jit_solution(4340860537249124590)
XLA Ops:
  0.6 61.6 %coarse_cycle.1 = (bf16[8,32,128]{2,1,0:T(8,128)(2,1)}, f32[1,1,2,4,32,128]{5,4,3,2,1,0:T(8,128)}) custom-call(s32[32]{0:T(128)} %owner_hbm.1, bf16[2,2,4,8,32,128]{5,4,3,2,1,0:T(8,128)(2,1)} %fine_ref.1, bf16[2,2,4,8,128,128]{5,4,3,2,1,0:T(8,128)(2,1)} %restr_ref.3, bf16[1,1,2,4,9,128,128]{6,5,4,3,2,1,0:T(8,128)(2,1)} %links_ref.1), custom_call_target="tpu_custom_call" | custom-call | tf_op jit(solution)/shard_map/coarse_cycle/pallas_call | solution.py:412
  62.2 5.3 %prolong.1 = (f32[2,2,4,8,32,128]{5,4,3,2,1,0:T(8,128)}, f32[1,1,2,4,32,128]{5,4,3,2,1,0:T(8,128)}) custom-call(bf16[8,32,128]{2,1,0:T(8,128)(2,1)} %get-tuple-element.4.fix_ref, f32[1,1,2,4,32,128]{5,4,3,2,1,0:T(8,128)} %get-tuple-element.5.res_in_ref, bf16[2,2,4,8,128,128]{5,4,3,2,1,0:T(8,128)(2,1)} %restr_ref.3), custom_call_target="tpu_custom_call" | custom-call | tf_op jit(solution)/shard_map/prolong/pallas_call | solution.py:454

commit v3 on v2

--- a/solution.py
+++ b/solution.py
@@ -36,7 +36,7 @@
     fine_v, restr_v, links_v, fix_v, res_v,
     own_v, mid_v, pick_v, r_v, low_v, p_v, img_v, orth_v,
     ph_v, lowh_v, imgh_v, rh_v,
-    midq0_v, midq1_v, pickq_v, backq_v, part_v, pair_v, sums_v, owner_ref, source_s,
+    qb_v, midb_v, pickb_v, back_v, part_v, pair_v, sums_v, owner_ref, source_s,
     owner_sem, fix_sem, res_sem, fine_sem, restr_sem, links_sem,
     up_send, up_recv, down_send, down_recv,
     p_send, p_recv, low_send, low_recv, img_send, img_recv,
@@ -47,9 +47,11 @@
     my_y, my_z = me // NZ, me % NZ
     my_x, my_c = tm // 2, tm % 2
 
+    by_z = [lax.rem(my_z + far_first(k, NZ), NZ) for k in range(NZ)]
+    by_y = [lax.rem(my_y + far_first(k, NY), NY) for k in range(NY)]
+
     def space_far(d):
-        dz, dy = far_first(d // NY, NZ), far_first(d % NY, NY)
-        return lax.rem(my_y + dy, NY) * NZ + lax.rem(my_z + dz, NZ)
+        return by_y[d % NY] * NZ + by_z[d // NY]
 
     def site_of(step):
         return lax.rem(my_z + far_first(step, NZ), CS)
@@ -105,12 +107,8 @@
     my_slot = my_z * 4 + my_y
     others = pl.ds(0, NS - 1)
 
-    def piece(d):
-        target = space_far(d)
-        return target, target % NZ * 4 + target // NZ
-
     for d in range(NS - 1):
-        target, slot = piece(d)
+        target, slot = space_far(d), by_z[d // NY] * 4 + by_y[d % NY]
         pltpu.make_async_remote_copy(
             src_ref=own_v.at[slot], dst_ref=mid_v.at[me],
             send_sem=up_send, recv_sem=up_recv,
@@ -144,27 +142,51 @@
     def read_imgh(it, k, cs):
         return imgh_v[it, k, pl.ds(4 * cs, 4)].reshape(RHS, W)
 
-    midq = (midq0_v, midq1_v)
+    parity = lax.rem(me, 2)
+    half_z = [lax.rem(my_z // 2 + k, NZ // 2) for k in (2, 1, 3, 0)]
 
     def back_up(it):
+        for cs in range(CS):
+            qb_v[it, pl.ds(2 * cs, 2)] = read_img(it, cs).astype(BF16).reshape(2, 16, W)
+        for d in range(16):
+            y, zh = by_y[d // 4], half_z[d % 4]
+            h = y * 4 + zh
+
+            def send(y=y, zh=zh, h=h):
+                pltpu.make_async_remote_copy(
+                    src_ref=qb_v.at[it, h], dst_ref=midb_v.at[me],
+                    send_sem=b1_send.at[it], recv_sem=b1_recv,
+                    device_id={"space": y * NZ + 2 * zh + it}, device_id_type=MESH).start()
+
+            if d < 15:
+                send()
+            else:
+                pl.when(parity != it)(send)
+
+                @pl.when(parity == it)
+                def _():
+                    midb_v[me] = qb_v[it, h]
+
+    def back_down():
+        drain(midb_v.at[others], b1_recv)
         for d in range(NS - 1):
-            target, slot = piece(d)
+            pickb_v[d] = midb_v[owner_ref[space_far(d)]]
+        for d in range(NS - 1):
             pltpu.make_async_remote_copy(
-                src_ref=img_v.at[it, slot], dst_ref=midq[it].at[me],
-                send_sem=b1_send.at[it], recv_sem=b1_recv.at[it],
-                device_id={"space": target}, device_id_type=MESH).start()
-        midq[it][me] = img_v[it, my_slot]
-
-    def back_down(it):
-        drain(midq[it].at[others], b1_recv.at[it])
-        for d in range(NS - 1):
-            target = space_far(d)
-            pickq_v[it, d] = midq[it][owner_ref[target]]
-            pltpu.make_async_remote_copy(
-                src_ref=pickq_v.at[it, d], dst_ref=backq_v.at[it, my_slot],
-                send_sem=b2_send.at[it], recv_sem=b2_recv.at[it],
-                device_id={"space": target}, device_id_type=MESH).start()
-        backq_v[it, my_slot] = midq[it][owner_ref[me]]
+                src_ref=pickb_v.at[d], dst_ref=back_v.at[parity, me // 2],
+                send_sem=b2_send, recv_sem=b2_recv.at[parity],
+                device_id={"space": space_far(d)}, device_id_type=MESH).start()
+        back_v[parity, me // 2] = midb_v[owner_ref[me]]
+
+    def drain_back(sems):
+        for it in range(2):
+            @pl.when(parity == it)
+            def _():
+                drain(back_v.at[it, pl.ds(0, 15)], sems.at[it])
+
+            @pl.when(parity != it)
+            def _():
+                drain(back_v.at[it], sems.at[it])
 
     halo_to = (
         {"tm": lax.rem(tm + NT - 1, NT)}, {"tm": lax.rem(tm + 1, NT)},
@@ -266,6 +288,8 @@
         pair_v[it, my_c] = mine
         pair = pair_copy(it)
         pair.start()
+        if it == 1:
+            back_up(0)
         pair.wait_recv()
         both = pair_v[it, 0] + pair_v[it, 1]
         part_v[it, 1] = both
@@ -274,10 +298,10 @@
         if it < 2:
             for k in range(4):
                 img_halo[it][k].start()
-        if it > 0:
-            back_down(it - 1)
-        if it < 2:
-            back_up(it)
+        if it == 1:
+            back_up(1)
+        if it == 2:
+            back_down()
         drain(sums_v.at[it, pl.ds(0, CHIPS - 1)], s_recv.at[it])
         totals = jnp.broadcast_to(jnp.sum(sums_v[it], axis=0), (RHS, W))
         cols = [
@@ -335,14 +359,14 @@
     wide = lambda c: jnp.broadcast_to(c, (RHS, W))
     w0, w1, w2 = wide(c0), wide(c1), wide(c2)
     s0, s1, b10 = wide(alphas[0]), wide(alphas[1]), wide(betas[1][0])
-    for it in range(2):
-        drain(backq_v.at[it, others], b2_recv.at[it])
+    drain_back(b2_recv)
     for cs in range(CS):
         sl = pl.ds(4 * cs, 4)
         r0 = own_v[sl].reshape(RHS, W)
-        q0 = backq_v[0, sl].reshape(RHS, W)
+        q0 = back_v[0, pl.ds(2 * cs, 2)].reshape(RHS, W).astype(F32)
+        q1 = back_v[1, pl.ds(2 * cs, 2)].reshape(RHS, W).astype(F32)
         r1 = r0 - s0 * q0
-        r2 = r1 - s1 * (backq_v[1, sl].reshape(RHS, W) - b10 * q0)
+        r2 = r1 - s1 * (q1 - b10 * q0)
         dirs = [r.astype(BF16).astype(F32) for r in (r0, r1, r2)]
         fix_v[cs] = (w0 * dirs[0] + w1 * dirs[1] + w2 * dirs[2]).astype(BF16)
 
@@ -359,15 +383,14 @@
     for it in range(ITERS):
         pair_copy(it).wait_send()
         drain(sums_v.at[it, pl.ds(0, CHIPS - 1)], s_send.at[it])
-    for it in range(2):
-        drain(midq[it].at[others], b1_send.at[it])
-        drain(pickq_v.at[it, others], b2_send.at[it])
+    drain_back(b1_send)
+    drain(pickb_v.at[others], b2_send)
     res_copy.wait()
     fix_copy.wait()
 
 
 def prolong_kernel(fix_ref, res_in_ref, restr_ref, corr_ref, res_ref,
-                   fix_v, restr_v, out_v, fix_sem, res_sem, restr_sem, out_sem):
+                   fix_v, res_v, restr_v, out_v, fix_sem, res_sem, restr_sem, out_sem):
     def views(cs):
         y, x = cs // 4, cs % 4
         return (slice(None), slice(None), pl.ds(2 * y, 2), pl.ds(2 * x, 2))
@@ -384,8 +407,9 @@
     ]
     for load in loads:
         load.start()
-    res_copy = pltpu.make_async_copy(res_in_ref, res_ref, res_sem)
-    res_copy.start()
+    res_in = pltpu.make_async_copy(res_in_ref, res_v, res_sem.at[0])
+    res_in.start()
+    res_out = pltpu.make_async_copy(res_v, res_ref, res_sem.at[1])
     fix_copy.wait()
     for cs in range(CS):
         loads[cs].wait()
@@ -399,7 +423,10 @@
                     out_v[cs, a, b, c, 0] = both[:, :W]
                     out_v[cs, a, b, c, 1] = both[:, W:]
         stores[cs].start()
-    res_copy.wait()
+        if cs == 0:
+            res_in.wait()
+            res_out.start()
+    res_out.wait()
     for store in stores:
         store.wait()
 
@@ -432,10 +459,10 @@
             pltpu.VMEM((4, CS, RHS, W), BF16),
             pltpu.VMEM((2, 4) + plane, F32),
             pltpu.VMEM((4, CS, RHS, W), F32),
-            pltpu.VMEM(plane, F32),
-            pltpu.VMEM(plane, F32),
-            pltpu.VMEM((2,) + plane, F32),
-            pltpu.VMEM((2,) + plane, F32),
+            pltpu.VMEM((2, 16, 16, W), BF16),
+            pltpu.VMEM((NS, 16, W), BF16),
+            pltpu.VMEM((NS, 16, W), BF16),
+            pltpu.VMEM((2, 16, 16, W), BF16),
             pltpu.VMEM((ITERS, 2, 1, W), F32),
             pltpu.VMEM((ITERS, 2, 1, W), F32),
             pltpu.VMEM((ITERS, CHIPS, 1, W), F32),
@@ -445,7 +472,7 @@
             dma(()), dma(()), dma(()), dma(()),
             dma((4,)), dma((4,)), dma((4,)), dma((4,)), dma((2, 4)), dma((2, 4)),
             dma((ITERS,)), dma((ITERS,)), dma((ITERS,)), dma((ITERS,)),
-            dma((2,)), dma((2,)), dma((2,)), dma((2,)),
+            dma((2,)), dma(()), dma(()), dma((2,)),
         ],
         compiler_params=pltpu.CompilerParams(
             collective_id=0, has_side_effects=True, vmem_limit_bytes=60 * MIB),
@@ -458,9 +485,10 @@
         out_specs=(hbm, hbm),
         scratch_shapes=[
             pltpu.VMEM((CS, RHS, W), BF16),
+            pltpu.VMEM((1, 1, 2, 4, RHS, W), F32),
             pltpu.VMEM((CS, 2, 2, 2, 2, W, W), BF16),
             pltpu.VMEM((CS, 2, 2, 2, 2, RHS, W), F32),
-            dma(()), dma(()), dma((CS,)), dma((CS,)),
+            dma(()), dma((2,)), dma((CS,)), dma((CS,)),
         ],
         compiler_params=pltpu.CompilerParams(vmem_limit_bytes=60 * MIB),
         name="prolong",

time: 67.6 us -> 62.7 us (0.928)
  Pallas kernels: 66.9 us -> 62 us
    pallas_call x1, Pallas kernels: 61.6 us -> 56.9 us  [body(): pl.pallas_call(cycle_kernel, out_shape=(jax.ShapeDtypeStruct((CS, RHS, W)...]
where the time goes in v3:
time: 62.7 us; the launch traced here: 62.6 us
  Pallas kernels  62 us (99%)
  between operations  0.64 us (1%)
    pallas_call x1, Pallas kernels, body(): pl.pallas_call(cycle_kernel, out_shape=(jax.ShapeDtypeStruct((CS, RHS, W)...  56.9 us
    pallas_call x1, Pallas kernels, body(): pl.pallas_call(prolong_kernel, out_shape=(jax.ShapeDtypeStruct(fine_resid...  5.06 us

profile of v3, /device:TPU:1, one launch (start us, length us, event | category | flops | bytes accessed | tf_op | source)
XLA Modules:
  0.0 62.6 jit_solution(11179648608697398917)
XLA Ops:
  0.6 56.9 %coarse_cycle.1 = (bf16[8,32,128]{2,1,0:T(8,128)(2,1)}, f32[1,1,2,4,32,128]{5,4,3,2,1,0:T(8,128)}) custom-call(s32[32]{0:T(128)} %owner_hbm.1, bf16[2,2,4,8,32,128]{5,4,3,2,1,0:T(8,128)(2,1)} %fine_ref.1, bf16[2,2,4,8,128,128]{5,4,3,2,1,0:T(8,128)(2,1)} %restr_ref.3, bf16[1,1,2,4,9,128,128]{6,5,4,3,2,1,0:T(8,128)(2,1)} %links_ref.1), custom_call_target="tpu_custom_call" | custom-call | tf_op jit(solution)/shard_map/coarse_cycle/pallas_call | solution.py:439
  57.6 5.1 %prolong.1 = (f32[2,2,4,8,32,128]{5,4,3,2,1,0:T(8,128)}, f32[1,1,2,4,32,128]{5,4,3,2,1,0:T(8,128)}) custom-call(bf16[8,32,128]{2,1,0:T(8,128)(2,1)} %get-tuple-element.4.fix_ref, f32[1,1,2,4,32,128]{5,4,3,2,1,0:T(8,128)} %get-tuple-element.5.res_in_ref, bf16[2,2,4,8,128,128]{5,4,3,2,1,0:T(8,128)(2,1)} %restr_ref.3), custom_call_target="tpu_custom_call" | custom-call | tf_op jit(solution)/shard_map/prolong/pallas_call | solution.py:481

commit v4 on v3

--- a/solution.py
+++ b/solution.py
@@ -53,8 +53,16 @@
     def space_far(d):
         return by_y[d % NY] * NZ + by_z[d // NY]
 
+    barrier = pltpu.get_barrier_semaphore()
+    for d in range(NS - 1):
+        pl.semaphore_signal(
+            barrier, inc=1, device_id={"space": space_far(d)}, device_id_type=MESH)
+    for d in (4, 5, 2, 3, 6, 7, 1):
+        pl.semaphore_signal(
+            barrier, inc=1, device_id={"tm": lax.rem(tm + d, NT)}, device_id_type=MESH)
+
     def site_of(step):
-        return lax.rem(my_z + far_first(step, NZ), CS)
+        return by_z[step]
 
     def fine_copies(step):
         cs = site_of(step)
@@ -72,14 +80,6 @@
             c.start()
     links_copy = pltpu.make_async_copy(links_ref.at[0, 0], links_v, links_sem)
     links_copy.start()
-
-    barrier = pltpu.get_barrier_semaphore()
-    for d in range(1, NS):
-        pl.semaphore_signal(
-            barrier, inc=1, device_id={"space": lax.rem(me + d, NS)}, device_id_type=MESH)
-    for d in range(1, NT):
-        pl.semaphore_signal(
-            barrier, inc=1, device_id={"tm": lax.rem(tm + d, NT)}, device_id_type=MESH)
 
     def find(z, carry):
         acc = jnp.int32(0)
@@ -117,8 +117,9 @@
     drain(mid_v.at[others], up_recv)
 
     for d in range(NS - 1):
+        pick_v[d] = mid_v[source_s[space_far(d)]]
+    for d in range(NS - 1):
         target = space_far(d)
-        pick_v[d] = mid_v[source_s[target]]
         pltpu.make_async_remote_copy(
             src_ref=pick_v.at[d], dst_ref=r_v.at[my_slot],
             send_sem=down_send, recv_sem=down_recv,
@@ -411,24 +412,26 @@
     res_in.start()
     res_out = pltpu.make_async_copy(res_v, res_ref, res_sem.at[1])
     fix_copy.wait()
-    for cs in range(CS):
-        loads[cs].wait()
-        fix = fix_v[cs]
-        for a in range(2):
-            for b in range(2):
-                for c in range(2):
-                    both = lax.dot_general(
-                        fix, restr_v[cs, a, b, c].reshape(2 * W, W),
-                        (((1,), (1,)), ((), ())), preferred_element_type=F32)
-                    out_v[cs, a, b, c, 0] = both[:, :W]
-                    out_v[cs, a, b, c, 1] = both[:, W:]
-        stores[cs].start()
-        if cs == 0:
-            res_in.wait()
-            res_out.start()
-    res_out.wait()
+    for group in ((0,), (1, 2), (3, 4), (5, 6), (7,)):
+        for cs in group:
+            loads[cs].wait()
+        for cs in group:
+            fix = fix_v[cs]
+            for a in range(2):
+                for b in range(2):
+                    for c in range(2):
+                        both = lax.dot_general(
+                            fix, restr_v[cs, a, b, c].reshape(2 * W, W),
+                            (((1,), (1,)), ((), ())), preferred_element_type=F32)
+                        out_v[cs, a, b, c, 0] = both[:, :W]
+                        out_v[cs, a, b, c, 1] = both[:, W:]
+        for cs in group:
+            stores[cs].start()
+    res_in.wait()
+    res_out.start()
     for store in stores:
         store.wait()
+    res_out.wait()
 
 
 def body(fine_residual, restriction, coarse_links, plane_owner):

time: 62.7 us -> 61.5 us (0.981)
  Pallas kernels: 62 us -> 60.8 us
    pallas_call x1, Pallas kernels: 5.06 us -> 3.98 us  [body(): pl.pallas_call(prolong_kernel, out_shape=(jax.ShapeDtypeStruct(fine_resid...]
where the time goes in v4:
time: 61.5 us; the launch traced here: 61.4 us
  Pallas kernels  60.8 us (99%)
  between operations  0.64 us (1%)
    pallas_call x1, Pallas kernels, body(): pl.pallas_call(cycle_kernel, out_shape=(jax.ShapeDtypeStruct((CS, RHS, W)...  56.8 us
    pallas_call x1, Pallas kernels, body(): pl.pallas_call(prolong_kernel, out_shape=(jax.ShapeDtypeStruct(fine_resid...  3.98 us

profile of v4, /device:TPU:1, one launch (start us, length us, event | category | flops | bytes accessed | tf_op | source)
XLA Modules:
  0.0 61.4 jit_solution(723394383232980959)
XLA Ops:
  0.6 56.8 %coarse_cycle.1 = (bf16[8,32,128]{2,1,0:T(8,128)(2,1)}, f32[1,1,2,4,32,128]{5,4,3,2,1,0:T(8,128)}) custom-call(s32[32]{0:T(128)} %owner_hbm.1, bf16[2,2,4,8,32,128]{5,4,3,2,1,0:T(8,128)(2,1)} %fine_ref.1, bf16[2,2,4,8,128,128]{5,4,3,2,1,0:T(8,128)(2,1)} %restr_ref.3, bf16[1,1,2,4,9,128,128]{6,5,4,3,2,1,0:T(8,128)(2,1)} %links_ref.1), custom_call_target="tpu_custom_call" | custom-call | tf_op jit(solution)/shard_map/coarse_cycle/pallas_call | solution.py:442
  57.4 4.0 %prolong.1 = (f32[2,2,4,8,32,128]{5,4,3,2,1,0:T(8,128)}, f32[1,1,2,4,32,128]{5,4,3,2,1,0:T(8,128)}) custom-call(bf16[8,32,128]{2,1,0:T(8,128)(2,1)} %get-tuple-element.4.fix_ref, f32[1,1,2,4,32,128]{5,4,3,2,1,0:T(8,128)} %get-tuple-element.5.res_in_ref, bf16[2,2,4,8,128,128]{5,4,3,2,1,0:T(8,128)(2,1)} %restr_ref.3), custom_call_target="tpu_custom_call" | custom-call | tf_op jit(solution)/shard_map/prolong/pallas_call | solution.py:484

commit v5 on v4

--- a/solution.py
+++ b/solution.py
@@ -254,26 +254,40 @@
         def outer(cs):
             return [ph_v[it, k, cs] for k in range(4)]
 
+        for cs in range(CS):
+            y, x = cs // 4, cs % 4
+            put_img(it, cs, dot(p_v[it, cs], links_v[y, x, 0]) + dot(
+                jnp.concatenate(inner(cs), axis=-1),
+                links_v[y, x, pl.ds(5, 4)].reshape(4 * W, W)))
         if it == 0:
-            for cs in range(CS):
-                y, x = cs // 4, cs % 4
-                put_img(it, cs, dot(p_v[it, cs], links_v[y, x, 0]) + dot(
-                    jnp.concatenate(inner(cs), axis=-1),
-                    links_v[y, x, pl.ds(5, 4)].reshape(4 * W, W)))
             for k in range(4):
                 p_halo[k].wait_recv()
+        else:
+            last = it - 1
+            coef = [jnp.broadcast_to(b, (RHS, W)) for b in betas[last]]
+            step = jnp.broadcast_to(alphas[last], (RHS, W))
+            for k in range(4):
+                if last == 0:
+                    low_halo[k].wait_recv()
+                img_halo[last][k].wait_recv()
+                for cs in range(CS):
+                    q = read_imgh(last, k, cs)
+                    if last == 0:
+                        old = ph_v[0, k, cs].astype(F32) + lowh_v[k, cs].astype(F32)
+                    else:
+                        old = rh_v[k, cs]
+                        q = q - coef[0] * read_imgh(0, k, cs)
+                    new = old - step * q
+                    if last == 0:
+                        rh_v[k, cs] = new
+                    ph_v[it, k, cs] = new.astype(BF16)
         nprod = it + 2
         prods = [jnp.zeros((RHS, W), F32) for _ in range(nprod)]
         for cs in range(CS):
             y, x = cs // 4, cs % 4
-            if it == 0:
-                q = read_img(it, cs) + dot(
-                    jnp.concatenate(outer(cs), axis=-1),
-                    links_v[y, x, pl.ds(1, 4)].reshape(4 * W, W))
-            else:
-                q = dot(
-                    jnp.concatenate([p_v[it, cs]] + outer(cs) + inner(cs), axis=-1),
-                    links_v[y, x].reshape(9 * W, W))
+            q = read_img(it, cs) + dot(
+                jnp.concatenate(outer(cs), axis=-1),
+                links_v[y, x, pl.ds(1, 4)].reshape(4 * W, W))
             put_img(it, cs, q)
             earlier = [read_img(0, cs), orth_v[cs]] if it == 2 else [read_img(0, cs)] * it
             factors = earlier + [q, read_r(cs)]
@@ -297,7 +311,7 @@
         sums_v[it, chip] = both
         send_chip(it)
         if it < 2:
-            for k in range(4):
+            for k in (2, 3, 0, 1):
                 img_halo[it][k].start()
         if it == 1:
             back_up(1)
@@ -333,22 +347,6 @@
                 p_v[it + 1, cs] = new.astype(BF16)
             else:
                 res_v[cs // 4, cs % 4] = new
-        if it < ITERS - 1:
-            for k in range(4):
-                if it == 0:
-                    low_halo[k].wait_recv()
-                img_halo[it][k].wait_recv()
-                for cs in range(CS):
-                    q = read_imgh(it, k, cs)
-                    if it == 0:
-                        old = ph_v[0, k, cs].astype(F32) + lowh_v[k, cs].astype(F32)
-                    else:
-                        old = rh_v[k, cs]
-                        q = q - coef[0] * read_imgh(0, k, cs)
-                    new = old - step * q
-                    if it == 0:
-                        rh_v[k, cs] = new
-                    ph_v[it + 1, k, cs] = new.astype(BF16)
 
     res_copy = pltpu.make_async_copy(res_v, res_ref.at[0, 0], res_sem)
     res_copy.start()

time: 61.5 us -> 61.6 us (level)
  no operation moved by 1% of the time
where the time goes in v5:
time: 61.6 us; the launch traced here: 61.5 us
  Pallas kernels  60.9 us (99%)
  between operations  0.64 us (1%)
    pallas_call x1, Pallas kernels, body(): pl.pallas_call(cycle_kernel, out_shape=(jax.ShapeDtypeStruct((CS, RHS, W)...  56.9 us
    pallas_call x1, Pallas kernels, body(): pl.pallas_call(prolong_kernel, out_shape=(jax.ShapeDtypeStruct(fine_resid...  3.98 us

profile of v5, /device:TPU:1, one launch (start us, length us, event | category | flops | bytes accessed | tf_op | source)
XLA Modules:
  0.0 61.5 jit_solution(8499748786996318721)
XLA Ops:
  0.6 56.9 %coarse_cycle.1 = (bf16[8,32,128]{2,1,0:T(8,128)(2,1)}, f32[1,1,2,4,32,128]{5,4,3,2,1,0:T(8,128)}) custom-call(s32[32]{0:T(128)} %owner_hbm.1, bf16[2,2,4,8,32,128]{5,4,3,2,1,0:T(8,128)(2,1)} %fine_ref.1, bf16[2,2,4,8,128,128]{5,4,3,2,1,0:T(8,128)(2,1)} %restr_ref.3, bf16[1,1,2,4,9,128,128]{6,5,4,3,2,1,0:T(8,128)(2,1)} %links_ref.1), custom_call_target="tpu_custom_call" | custom-call | tf_op jit(solution)/shard_map/coarse_cycle/pallas_call | solution.py:440
  57.6 4.0 %prolong.1 = (f32[2,2,4,8,32,128]{5,4,3,2,1,0:T(8,128)}, f32[1,1,2,4,32,128]{5,4,3,2,1,0:T(8,128)}) custom-call(bf16[8,32,128]{2,1,0:T(8,128)(2,1)} %get-tuple-element.4.fix_ref, f32[1,1,2,4,32,128]{5,4,3,2,1,0:T(8,128)} %get-tuple-element.5.res_in_ref, bf16[2,2,4,8,128,128]{5,4,3,2,1,0:T(8,128)(2,1)} %restr_ref.3), custom_call_target="tpu_custom_call" | custom-call | tf_op jit(solution)/shard_map/prolong/pallas_call | solution.py:482
